TPU v7x, 32 devices: a whole 2x2x4 slice. The times are simulated.
32 devices in a mesh: ctx: 8 (over z, y), head: 4 (over x, core).
Axes of the slice: x: 2, y: 2, z: 4, core: 2. Of those that a mesh axis runs over, the one named last changes fastest.
Arguments:
- queries: bfloat16 [2048, 2048], P('ctx', 'head'), may hold values from -6 to 6
- keys: bfloat16 [2048, 2048], P('ctx', 'head'), may hold values from -6 to 6
- values: bfloat16 [2048, 2048], P('ctx', 'head'), may hold values from -6 to 6
- out_grad: bfloat16 [2048, 2048], P('ctx', 'head'), may hold values from -6 to 6
- doc_lengths: int32 [8], replicated, may hold values from 1 to 768, as said below
Outputs:
- attended: float32 [2048, 2048], P('ctx', 'head')
- query_grad: float32 [2048, 2048], P('ctx', 'head')
- key_grad: float32 [2048, 2048], P('ctx', 'head')
- value_grad: float32 [2048, 2048], P('ctx', 'head')
Inputs may be any that keep to these rules, and one draw needn't show every extreme that they name: `doc_lengths`: the first document has exactly 768 tokens, every other one 1 to 768, and all lengths sum to 2048.
All inputs are finite; a program needn't handle non-finite values.
Results may differ from a plain program's by a relative error of at most 0.0095.
Values may be sent and summed in bfloat16 or wider, within the bound.
A program may use at most 64 MiB of HBM per device.

v0:
```python
import math

import jax
import jax.numpy as jnp
from jax import lax
from jax.sharding import PartitionSpec as P

HD = 128
PROMPT = 64


NEG_FILL = -1e30


def from_root(value, axis, source):
    kept = jnp.where(lax.axis_index(axis) == source, value, 0).astype(value.dtype)
    return lax.psum(kept, axis)


def passed_along(block, axis, distance):
    devices = range(lax.axis_size(axis))
    route = [(i - distance, i) for i in devices if i - distance in devices]
    return lax.ppermute(block, axis, route)


def shifted(value, axis, by):
    length = lax.axis_size(axis)
    return lax.ppermute(value, axis, [(i, (i + by) % length) for i in range(length)])


def on_device(queries, keys, values, out_grad, doc_lengths):
    tok_rows = queries.shape[0]
    feat_width = queries.shape[1]
    heads_here = feat_width // HD
    ctx_count = lax.axis_size("ctx")
    reach = min(3, ctx_count // 2 - 1)
    own_block = lax.axis_index("ctx")
    score_scale = 1.0 / math.sqrt(HD)
    doc_ends = jnp.cumsum(doc_lengths)
    offsets = jnp.arange(tok_rows, dtype=jnp.int32)
    prompt_pos = jnp.arange(PROMPT, dtype=jnp.int32)
    q_three = queries.reshape(tok_rows, heads_here, HD)
    k_three = keys.reshape(tok_rows, heads_here, HD)
    v_three = values.reshape(tok_rows, heads_here, HD)
    dout_three = out_grad.reshape(tok_rows, heads_here, HD)
    prompt_k, prompt_v = (
        from_root(k_three[:PROMPT], "ctx", 0),
        from_root(v_three[:PROMPT], "ctx", 0),
    )

    def block_segments(block):
        positions = block * tok_rows + offsets
        return jnp.sum((doc_ends[None, :] <= positions[:, None]).astype(jnp.int32), axis=1)

    def tile_scores(query_rows, key_rows, query_block, key_block):
        scores = (
            jnp.einsum("thd,uhd->htu", query_rows, key_rows, preferred_element_type=jnp.float32)
            * score_scale
        )
        query_pos = query_block * tok_rows + offsets
        key_pos = key_block * tok_rows + offsets
        same_doc = block_segments(query_block)[:, None] == block_segments(key_block)[None, :]
        allowed = (key_pos[None, :] <= query_pos[:, None]) & same_doc & (key_pos[None, :] >= PROMPT)
        return (scores, allowed)

    def fold_scored(partial_value, scores, allowed, value_rows):
        running, totals, accum = partial_value
        row_top = jnp.max(jnp.where(allowed[None], scores, NEG_FILL), axis=2)
        newest = jnp.maximum(running, row_top)
        fading = jnp.exp(running - newest)
        weights = jnp.where(allowed[None], jnp.exp(scores - newest[:, :, None]), 0.0)
        totals = totals * fading + jnp.sum(weights, axis=2)
        added = jnp.einsum(
            "htu,uhd->thd", weights, value_rows.astype(jnp.float32), precision=lax.Precision.HIGHEST
        )
        accum = accum * fading.T[:, :, None] + added
        return (newest, totals, accum)

    def fold_tile(partial_value, query_rows, key_rows, value_rows, query_block, key_block):
        scores, allowed = tile_scores(query_rows, key_rows, query_block, key_block)
        return fold_scored(partial_value, scores, allowed, value_rows)

    def guarded_fold(partial_value, query_rows, key_rows, value_rows, query_block, key_block):
        return fold_tile(partial_value, query_rows, key_rows, value_rows, query_block, key_block)

    empty_partial = (
        jnp.full((heads_here, tok_rows), NEG_FILL, jnp.float32),
        jnp.zeros((heads_here, tok_rows), jnp.float32),
        jnp.zeros((tok_rows, heads_here, HD), jnp.float32),
    )
    scores = (
        jnp.einsum("thd,uhd->htu", q_three, prompt_k, preferred_element_type=jnp.float32)
        * score_scale
    )
    query_pos = own_block * tok_rows + offsets
    allowed = prompt_pos[None, :] <= query_pos[:, None]
    p_scores = scores
    p_allowed = allowed
    prompt_partial = fold_scored(empty_partial, p_scores, p_allowed, prompt_v)
    partial_value = fold_tile(prompt_partial, q_three, k_three, v_three, own_block, own_block)

    def forward_turn(distance, carried):
        key_rows, value_rows, running, totals, accum = carried
        key_rows, value_rows = passed_along((key_rows, value_rows), "ctx", 1)
        key_block = (own_block - distance) % ctx_count
        running, totals, accum = guarded_fold(
            (running, totals, accum), q_three, key_rows, value_rows, own_block, key_block
        )
        return (key_rows, value_rows, running, totals, accum)

    looped = lax.fori_loop(1, reach + 1, forward_turn, (k_three, v_three) + partial_value)
    running, totals, accum = (looped[2], looped[3], looped[4])
    attended_three = accum / totals.T[:, :, None]
    lse_rows = running + jnp.log(totals)
    delta_rows = jnp.sum(dout_three.astype(jnp.float32) * attended_three, axis=2).T

    def grad_scored(
        query_rows, dout_rows, lse_part, delta_part, key_rows, value_rows, scores, allowed
    ):
        weights = jnp.where(allowed[None], jnp.exp(scores - lse_part[:, :, None]), 0.0)
        rounded = weights.astype(jnp.bfloat16)
        value_part = jnp.einsum(
            "htu,thd->uhd", rounded, dout_rows, preferred_element_type=jnp.float32
        )
        dprob = jnp.einsum(
            "thd,uhd->htu", dout_rows, value_rows, preferred_element_type=jnp.float32
        )
        dscore = (weights * (dprob - delta_part[:, :, None])).astype(jnp.bfloat16)
        query_part = jnp.einsum(
            "htu,uhd->thd", dscore, key_rows, preferred_element_type=jnp.float32
        )
        key_part = jnp.einsum(
            "htu,thd->uhd", dscore, query_rows, preferred_element_type=jnp.float32
        )
        return (query_part, key_part, value_part)

    def grad_tile(
        query_rows, dout_rows, lse_part, delta_part, key_rows, value_rows, query_block, key_block
    ):
        scores, allowed = tile_scores(query_rows, key_rows, query_block, key_block)
        return grad_scored(
            query_rows, dout_rows, lse_part, delta_part, key_rows, value_rows, scores, allowed
        )

    def guarded_grad(
        query_rows, dout_rows, lse_part, delta_part, key_rows, value_rows, query_block, key_block
    ):
        return grad_tile(
            query_rows,
            dout_rows,
            lse_part,
            delta_part,
            key_rows,
            value_rows,
            query_block,
            key_block,
        )

    prompt_q, prompt_dk, prompt_dv = grad_scored(
        q_three, dout_three, lse_rows, delta_rows, prompt_k, prompt_v, p_scores, p_allowed
    )
    prompt_dk, prompt_dv = lax.psum((prompt_dk, prompt_dv), "ctx")
    own_grads = grad_tile(
        q_three, dout_three, lse_rows, delta_rows, k_three, v_three, own_block, own_block
    )
    home_grads = (own_grads[0] + prompt_q, own_grads[1], own_grads[2])

    def key_turn(distance, carried):
        key_rows, value_rows, query_acc, key_acc, value_acc = carried
        key_rows, value_rows = passed_along((key_rows, value_rows), "ctx", 1)
        key_acc, value_acc = (
            shifted(key_acc.astype(jnp.bfloat16), "ctx", 1).astype(key_acc.dtype),
            shifted(value_acc.astype(jnp.bfloat16), "ctx", 1).astype(value_acc.dtype),
        )
        key_block = (own_block - distance) % ctx_count
        parts = guarded_grad(
            q_three, dout_three, lse_rows, delta_rows, key_rows, value_rows, own_block, key_block
        )
        return (
            key_rows,
            value_rows,
            query_acc + parts[0],
            key_acc + parts[1],
            value_acc + parts[2],
        )

    looped = lax.fori_loop(1, reach + 1, key_turn, (k_three, v_three) + home_grads)
    query_acc = looped[2]
    key_acc, value_acc = (
        shifted(looped[3].astype(jnp.bfloat16), "ctx", -reach).astype(jnp.float32),
        shifted(looped[4].astype(jnp.bfloat16), "ctx", -reach).astype(jnp.float32),
    )
    first_block = own_block == 0
    key_acc = key_acc.at[:PROMPT].add(jnp.where(first_block, prompt_dk, 0.0))
    value_acc = value_acc.at[:PROMPT].add(jnp.where(first_block, prompt_dv, 0.0))
    attended = attended_three.reshape(tok_rows, feat_width)
    query_grad = (query_acc * score_scale).reshape(tok_rows, feat_width)
    key_grad = (key_acc * score_scale).reshape(tok_rows, feat_width)
    value_grad = value_acc.reshape(tok_rows, feat_width)
    return (attended, query_grad, key_grad, value_grad)


def solution(mesh):
    in_specs = (P("ctx", "head"), P("ctx", "head"), P("ctx", "head"), P("ctx", "head"), P())
    out_specs = (P("ctx", "head"), P("ctx", "head"), P("ctx", "head"), P("ctx", "head"))
    return jax.shard_map(
        on_device, mesh=mesh, in_specs=in_specs, out_specs=out_specs, check_vma=False
    )
```

profile of v0, /device:TPU:0, one launch (start us, length us, event | category | flops | bytes accessed | tf_op | source)
XLA Modules:
  0.0 302.5 jit_solution(6971112553658971312)
XLA Ops:
  7.2 0.9 select_bitcast_fusion
  9.7 0.8 copy-done.9
  10.6 0.7 copy-done.17
  15.1 69.0 %all-reduce.7.cloned.1.call-done = (bf16[64,4,128]{2,0,1:T(8,128)(2,1)}, bf16[64,4,128]{2,0,1:T(8,128)(2,1)}) async-done(((bf16[64,4,128]{2,0,1:T(8,128)(2,1)}, bf16[64,4,128]{2,0,1:T(8,128)(2,1)}), (bf16[64,4,128]{2,0,1:T(8,128)(2,1)}, bf16[64,4,128]{2,0,1:T(8,128)(2,1)})) %all-reduce.7.cloned.1.call-update) | async-done | bytes 131088 | tf_op jit(solution)/shard_map/psum | solution.py:17
  84.1 1.0 select_reduce_fusion.2
  85.4 0.8 copy-done.11
  87.5 46.2 %while.52 = (s32[]{:T(128)}, bf16[256,4,128]{2,0,1:T(8,128)(2,1)}, bf16[256,4,128]{2,0,1:T(8,128)(2,1)}, f32[4,256]{1,0:T(4,128)S(1)}, f32[4,256]{1,0:T(4,128)S(...) while((s32[]{:T(128)}, bf16[256,4,128]{2,0,1:T(8,128)(2,1)}, ...), condition=%wide.region_13.14_spmd.clone.clone, body=%wide.region_8.13_spmd.clone.clone.sunk | while | flops 472399360 | bytes 8465294 | solution.py:111
  87.5 2.7 collective-permute-start
  90.2 3.6 %collective-permute-start.1 = (bf16[256,4,128]{2,0,1:T(8,128)(2,1)}, bf16[256,4,128]{2,0,1:T(8,128)(2,1)S(1)}, u32[]{:S(2)}, u32[]{:S(2)}) collective-permute-start(bf16[256,4,128]{2,0,1:T(8,128)(2,1)} %get-tuple-element.1029), channel_id=1, source_target_pairs={{0,4},{4,8},{8,12},{12,16},{16,20},{20,24},{24,28},{1,5},{5,9},{9,... | collective-permute-start | bytes 786440 | tf_op jit(solution)/shard_map/while/body/eval_jaxpr/ppermute | solution.py:23
  94.1 2.7 collective-permute-done
  98.2 1.9 collective-permute-done.1
  100.7 1.1 fusion.111
  101.9 4.3 %collective-permute-start = (bf16[256,4,128]{2,0,1:T(8,128)(2,1)}, bf16[256,4,128]{2,0,1:T(8,128)(2,1)S(1)}, u32[]{:S(2)}, u32[]{:S(2)}) collective-permute-start(bf16[256,4,128]{2,0,1:T(8,128)(2,1)} %get-tuple-element.1028), channel_id=1, source_target_pairs={{0,4},{4,8},{8,12},{12,16},{16,20},{20,24},{24,28},{1,5},{5,9},{9,... | collective-permute-start | bytes 786440 | tf_op jit(solution)/shard_map/while/body/eval_jaxpr/ppermute | solution.py:23
  106.2 4.5 %collective-permute-start.1 = (bf16[256,4,128]{2,0,1:T(8,128)(2,1)}, bf16[256,4,128]{2,0,1:T(8,128)(2,1)S(1)}, u32[]{:S(2)}, u32[]{:S(2)}) collective-permute-start(bf16[256,4,128]{2,0,1:T(8,128)(2,1)} %get-tuple-element.1029), channel_id=1, source_target_pairs={{0,4},{4,8},{8,12},{12,16},{16,20},{20,24},{24,28},{1,5},{5,9},{9,... | collective-permute-start | bytes 786440 | tf_op jit(solution)/shard_map/while/body/eval_jaxpr/ppermute | solution.py:23
  111.0 1.5 collective-permute-done
  113.7 2.2 collective-permute-done.1
  116.7 1.1 fusion.111
  117.8 4.3 %collective-permute-start = (bf16[256,4,128]{2,0,1:T(8,128)(2,1)}, bf16[256,4,128]{2,0,1:T(8,128)(2,1)S(1)}, u32[]{:S(2)}, u32[]{:S(2)}) collective-permute-start(bf16[256,4,128]{2,0,1:T(8,128)(2,1)} %get-tuple-element.1028), channel_id=1, source_target_pairs={{0,4},{4,8},{8,12},{12,16},{16,20},{20,24},{24,28},{1,5},{5,9},{9,... | collective-permute-start | bytes 786440 | tf_op jit(solution)/shard_map/while/body/eval_jaxpr/ppermute | solution.py:23
  122.1 4.7 %collective-permute-start.1 = (bf16[256,4,128]{2,0,1:T(8,128)(2,1)}, bf16[256,4,128]{2,0,1:T(8,128)(2,1)S(1)}, u32[]{:S(2)}, u32[]{:S(2)}) collective-permute-start(bf16[256,4,128]{2,0,1:T(8,128)(2,1)} %get-tuple-element.1029), channel_id=1, source_target_pairs={{0,4},{4,8},{8,12},{12,16},{16,20},{20,24},{24,28},{1,5},{5,9},{9,... | collective-permute-start | bytes 786440 | tf_op jit(solution)/shard_map/while/body/eval_jaxpr/ppermute | solution.py:23
  127.2 1.8 collective-permute-done
  130.3 1.6 collective-permute-done.1
  132.6 1.1 fusion.111
  133.8 0.9 convolution_bitcast_fusion.10
  134.7 1.0 convolution_bitcast_fusion.4
  136.0 0.7 copy-done.12
  136.9 0.8 copy-done.3
  139.0 1.0 convolution_bitcast_fusion.5
  141.0 73.4 %while.53 = (s32[]{:T(128)}, bf16[256,4,128]{2,0,1:T(8,128)(2,1)S(1)}, bf16[256,4,128]{2,0,1:T(8,128)(2,1)S(1)}, f32[256,4,128]{2,0,1:T(8,128)S(1)}, bf16[256,4,...) while((s32[]{:T(128)}, ...), condition=%wide.region_18.19_spmd.clone.clone, body=%wide.region_15.18_spmd.clone.clone.sunk | while | flops 338571776 | bytes 14044150 | solution.py:187
  141.0 4.3 %collective-permute-start.2 = (bf16[256,4,128]{2,0,1:T(8,128)(2,1)S(1)}, bf16[256,4,128]{2,0,1:T(8,128)(2,1)S(1)}, u32[]{:S(2)}, u32[]{:S(2)}) collective-permute-start(bf16[256,4,128]{2,0,1:T(8,128)(2,1)S(1)} %get-tuple-element.1076), channel_id=1, source_target_pairs={{0,4},{4,8},{8,12},{12,16},{16,20},{20,24},{24,28},{1,5},{5,9},{9,... | collective-permute-start | bytes 786440 | tf_op jit(solution)/shard_map/while/body/eval_jaxpr/ppermute | solution.py:23
  145.3 4.1 %collective-permute-start.3 = (bf16[256,4,128]{2,0,1:T(8,128)(2,1)S(1)}, bf16[256,4,128]{2,0,1:T(8,128)(2,1)S(1)}, u32[]{:S(2)}, u32[]{:S(2)}) collective-permute-start(bf16[256,4,128]{2,0,1:T(8,128)(2,1)S(1)} %get-tuple-element.1077), channel_id=1, source_target_pairs={{0,4},{4,8},{8,12},{12,16},{16,20},{20,24},{24,28},{1,5},{5,9},{9,... | collective-permute-start | bytes 786440 | tf_op jit(solution)/shard_map/while/body/eval_jaxpr/ppermute | solution.py:23
  149.5 2.0 collective-permute-start.5
  152.4 5.2 %collective-permute-done.3 = bf16[256,4,128]{2,0,1:T(8,128)(2,1)S(1)} collective-permute-done((bf16[256,4,128]{2,0,1:T(8,128)(2,1)S(1)}, bf16[256,4,128]{2,0,1:T(8,128)(2,1)S(1)}, u32[]{:S(2)}, u32[]{:S(2)}) %collective-permute-start.3) | collective-permute-done | bytes 262176 | tf_op jit(solution)/shard_map/while/body/eval_jaxpr/ppermute | solution.py:23
  158.3 4.2 %collective-permute-done.4 = bf16[256,4,128]{2,0,1:T(8,128)(2,1)S(1)} collective-permute-done((bf16[256,4,128]{2,0,1:T(8,128)(2,1)}, bf16[256,4,128]{2,0,1:T(8,128)(2,1)S(1)}, u32[]{:S(2)}, u32[]{:S(2)}) %collective-permute-start.4) | collective-permute-done | bytes 262176 | tf_op jit(solution)/shard_map/while/body/eval_jaxpr/ppermute | solution.py:28
  162.5 1.0 convert_add_fusion.4
  163.6 1.8 collective-permute-done.5
  165.4 1.0 convert_add_fusion.5
  166.4 4.3 %collective-permute-start.2 = (bf16[256,4,128]{2,0,1:T(8,128)(2,1)S(1)}, bf16[256,4,128]{2,0,1:T(8,128)(2,1)S(1)}, u32[]{:S(2)}, u32[]{:S(2)}) collective-permute-start(bf16[256,4,128]{2,0,1:T(8,128)(2,1)S(1)} %get-tuple-element.1076), channel_id=1, source_target_pairs={{0,4},{4,8},{8,12},{12,16},{16,20},{20,24},{24,28},{1,5},{5,9},{9,... | collective-permute-start | bytes 786440 | tf_op jit(solution)/shard_map/while/body/eval_jaxpr/ppermute | solution.py:23
  170.7 3.3 %collective-permute-start.3 = (bf16[256,4,128]{2,0,1:T(8,128)(2,1)S(1)}, bf16[256,4,128]{2,0,1:T(8,128)(2,1)S(1)}, u32[]{:S(2)}, u32[]{:S(2)}) collective-permute-start(bf16[256,4,128]{2,0,1:T(8,128)(2,1)S(1)} %get-tuple-element.1077), channel_id=1, source_target_pairs={{0,4},{4,8},{8,12},{12,16},{16,20},{20,24},{24,28},{1,5},{5,9},{9,... | collective-permute-start | bytes 786440 | tf_op jit(solution)/shard_map/while/body/eval_jaxpr/ppermute | solution.py:23
  174.0 1.8 collective-permute-start.5
  176.1 1.3 collective-permute-done.2
  177.8 5.2 %collective-permute-done.3 = bf16[256,4,128]{2,0,1:T(8,128)(2,1)S(1)} collective-permute-done((bf16[256,4,128]{2,0,1:T(8,128)(2,1)S(1)}, bf16[256,4,128]{2,0,1:T(8,128)(2,1)S(1)}, u32[]{:S(2)}, u32[]{:S(2)}) %collective-permute-start.3) | collective-permute-done | bytes 262176 | tf_op jit(solution)/shard_map/while/body/eval_jaxpr/ppermute | solution.py:23
  183.7 3.3 %collective-permute-done.4 = bf16[256,4,128]{2,0,1:T(8,128)(2,1)S(1)} collective-permute-done((bf16[256,4,128]{2,0,1:T(8,128)(2,1)}, bf16[256,4,128]{2,0,1:T(8,128)(2,1)S(1)}, u32[]{:S(2)}, u32[]{:S(2)}) %collective-permute-start.4) | collective-permute-done | bytes 262176 | tf_op jit(solution)/shard_map/while/body/eval_jaxpr/ppermute | solution.py:28
  187.0 1.1 convert_add_fusion.4
  188.1 1.8 collective-permute-done.5
  189.8 1.0 convert_add_fusion.5
  190.9 4.3 %collective-permute-start.2 = (bf16[256,4,128]{2,0,1:T(8,128)(2,1)S(1)}, bf16[256,4,128]{2,0,1:T(8,128)(2,1)S(1)}, u32[]{:S(2)}, u32[]{:S(2)}) collective-permute-start(bf16[256,4,128]{2,0,1:T(8,128)(2,1)S(1)} %get-tuple-element.1076), channel_id=1, source_target_pairs={{0,4},{4,8},{8,12},{12,16},{16,20},{20,24},{24,28},{1,5},{5,9},{9,... | collective-permute-start | bytes 786440 | tf_op jit(solution)/shard_map/while/body/eval_jaxpr/ppermute | solution.py:23
  195.2 3.1 %collective-permute-start.3 = (bf16[256,4,128]{2,0,1:T(8,128)(2,1)S(1)}, bf16[256,4,128]{2,0,1:T(8,128)(2,1)S(1)}, u32[]{:S(2)}, u32[]{:S(2)}) collective-permute-start(bf16[256,4,128]{2,0,1:T(8,128)(2,1)S(1)} %get-tuple-element.1077), channel_id=1, source_target_pairs={{0,4},{4,8},{8,12},{12,16},{16,20},{20,24},{24,28},{1,5},{5,9},{9,... | collective-permute-start | bytes 786440 | tf_op jit(solution)/shard_map/while/body/eval_jaxpr/ppermute | solution.py:23
  198.3 0.9 collective-permute-start.5
  199.5 2.4 collective-permute-done.2
  202.3 5.2 %collective-permute-done.3 = bf16[256,4,128]{2,0,1:T(8,128)(2,1)S(1)} collective-permute-done((bf16[256,4,128]{2,0,1:T(8,128)(2,1)S(1)}, bf16[256,4,128]{2,0,1:T(8,128)(2,1)S(1)}, u32[]{:S(2)}, u32[]{:S(2)}) %collective-permute-start.3) | collective-permute-done | bytes 262176 | tf_op jit(solution)/shard_map/while/body/eval_jaxpr/ppermute | solution.py:23
  208.2 2.4 collective-permute-done.4
  210.6 1.1 convert_add_fusion.4
  211.6 1.8 collective-permute-done.5
  213.4 1.1 convert_add_fusion.5
  214.4 0.9 convolution_bitcast_fusion.11
  215.3 0.9 copy-done.15
  216.2 6.7 %collective-permute-start.6 = (bf16[256,4,128]{2,0,1:T(8,128)(2,1)S(1)}, bf16[256,4,128]{2,0,1:T(8,128)(2,1)S(1)}, u32[]{:S(2)}, u32[]{:S(2)}) collective-permute-start(bf16[256,4,128]{2,0,1:T(8,128)(2,1)S(1)} %copy-done.15), channel_id=1, source_target_pairs={{0,20},{4,24},{8,28},{12,0},{16,4},{20,8},{24,12},{28,16},{1,21},{... | collective-permute-start | bytes 786440 | tf_op jit(solution)/shard_map/ppermute | solution.py:28
  223.2 1.0 copy.100
  224.2 1.0 copy.99
  225.3 66.1 %all-reduce.5.cloned.1.call-done = (f32[64,4,128]{2,0,1:T(8,128)}, f32[64,4,128]{2,0,1:T(8,128)}) async-done(((f32[64,4,128]{2,0,1:T(8,128)}, f32[64,4,128]{2,0,1:T(8,128)}), (f32[64,4,128]{2,0,1:T(8,128)}, f32[64,4,128]{2,0,1:T(8,128)})) %all-reduce.5.cloned.1.call-update) | async-done | bytes 262160 | tf_op jit(solution)/shard_map/psum | solution.py:162
  291.4 0.9 fusion.40
  292.5 1.0 copy.102
  293.5 0.9 copy-done.16
  294.7 1.0 copy.101
  (145 shorter events, 21.5 us)
Async XLA Ops:
  7.2 76.9 %all-reduce.7.cloned.1.call-start = ((), (), s32[]{:S(2)}) async-start(), calls=%async_computation.1 | async-start | bytes 262144 | tf_op jit(solution)/shard_map/psum | solution.py:17
  8.1 1.4 copy-start.8
  9.4 281.9 %all-reduce.5.cloned.1.call-start = ((), (), s32[]{:S(2)}) async-start(), calls=%async_computation | async-start | bytes 524288 | tf_op jit(solution)/shard_map/psum | solution.py:162
  9.5 1.0 copy-start.9
  10.5 1.9 copy-start
  10.5 1.1 copy-start.13
  10.6 76.0 %copy-start.2 = (bf16[256,512]{0,1:T(8,128)(2,1)}, bf16[256,512]{0,1:T(8,128)(2,1)S(1)}, u32[]{:S(2)}) copy-start(bf16[256,512]{0,1:T(8,128)(2,1)S(1)} %copy.65) | copy-start | bytes 786436
  10.6 0.7 copy-start.17
  12.0 0.7 copy-start.4
  13.6 0.8 copy-start.6
  13.6 1.1 copy-start.14
  85.3 0.8 copy-start.11
  87.5 9.3 %collective-permute-start = (bf16[256,4,128]{2,0,1:T(8,128)(2,1)}, bf16[256,4,128]{2,0,1:T(8,128)(2,1)S(1)}, u32[]{:S(2)}, u32[]{:S(2)}) collective-permute-start(bf16[256,4,128]{2,0,1:T(8,128)(2,1)} %get-tuple-element.1028), channel_id=1, source_target_pairs={{0,4},{4,8},{8,12},{12,16},{16,20},{20,24},{24,28},{1,5},{5,9},{9,... | collective-permute-start | bytes 786440 | tf_op jit(solution)/shard_map/while/body/eval_jaxpr/ppermute | solution.py:23
  90.2 9.8 %collective-permute-start.1 = (bf16[256,4,128]{2,0,1:T(8,128)(2,1)}, bf16[256,4,128]{2,0,1:T(8,128)(2,1)S(1)}, u32[]{:S(2)}, u32[]{:S(2)}) collective-permute-start(bf16[256,4,128]{2,0,1:T(8,128)(2,1)} %get-tuple-element.1029), channel_id=1, source_target_pairs={{0,4},{4,8},{8,12},{12,16},{16,20},{20,24},{24,28},{1,5},{5,9},{9,... | collective-permute-start | bytes 786440 | tf_op jit(solution)/shard_map/while/body/eval_jaxpr/ppermute | solution.py:23
  101.9 10.6 %collective-permute-start = (bf16[256,4,128]{2,0,1:T(8,128)(2,1)}, bf16[256,4,128]{2,0,1:T(8,128)(2,1)S(1)}, u32[]{:S(2)}, u32[]{:S(2)}) collective-permute-start(bf16[256,4,128]{2,0,1:T(8,128)(2,1)} %get-tuple-element.1028), channel_id=1, source_target_pairs={{0,4},{4,8},{8,12},{12,16},{16,20},{20,24},{24,28},{1,5},{5,9},{9,... | collective-permute-start | bytes 786440 | tf_op jit(solution)/shard_map/while/body/eval_jaxpr/ppermute | solution.py:23
  106.2 9.8 %collective-permute-start.1 = (bf16[256,4,128]{2,0,1:T(8,128)(2,1)}, bf16[256,4,128]{2,0,1:T(8,128)(2,1)S(1)}, u32[]{:S(2)}, u32[]{:S(2)}) collective-permute-start(bf16[256,4,128]{2,0,1:T(8,128)(2,1)} %get-tuple-element.1029), channel_id=1, source_target_pairs={{0,4},{4,8},{8,12},{12,16},{16,20},{20,24},{24,28},{1,5},{5,9},{9,... | collective-permute-start | bytes 786440 | tf_op jit(solution)/shard_map/while/body/eval_jaxpr/ppermute | solution.py:23
  117.8 11.2 %collective-permute-start = (bf16[256,4,128]{2,0,1:T(8,128)(2,1)}, bf16[256,4,128]{2,0,1:T(8,128)(2,1)S(1)}, u32[]{:S(2)}, u32[]{:S(2)}) collective-permute-start(bf16[256,4,128]{2,0,1:T(8,128)(2,1)} %get-tuple-element.1028), channel_id=1, source_target_pairs={{0,4},{4,8},{8,12},{12,16},{16,20},{20,24},{24,28},{1,5},{5,9},{9,... | collective-permute-start | bytes 786440 | tf_op jit(solution)/shard_map/while/body/eval_jaxpr/ppermute | solution.py:23
  122.1 9.8 %collective-permute-start.1 = (bf16[256,4,128]{2,0,1:T(8,128)(2,1)}, bf16[256,4,128]{2,0,1:T(8,128)(2,1)S(1)}, u32[]{:S(2)}, u32[]{:S(2)}) collective-permute-start(bf16[256,4,128]{2,0,1:T(8,128)(2,1)} %get-tuple-element.1029), channel_id=1, source_target_pairs={{0,4},{4,8},{8,12},{12,16},{16,20},{20,24},{24,28},{1,5},{5,9},{9,... | collective-permute-start | bytes 786440 | tf_op jit(solution)/shard_map/while/body/eval_jaxpr/ppermute | solution.py:23
  135.9 0.8 copy-start.12
  136.7 0.9 copy-start.3
  137.7 0.9 copy-start.1
  139.0 1.0 copy-start.10
  140.0 1.0 copy-start.5
  140.0 1.0 copy-start.7
  141.0 11.0 %collective-permute-start.2 = (bf16[256,4,128]{2,0,1:T(8,128)(2,1)S(1)}, bf16[256,4,128]{2,0,1:T(8,128)(2,1)S(1)}, u32[]{:S(2)}, u32[]{:S(2)}) collective-permute-start(bf16[256,4,128]{2,0,1:T(8,128)(2,1)S(1)} %get-tuple-element.1076), channel_id=1, source_target_pairs={{0,4},{4,8},{8,12},{12,16},{16,20},{20,24},{24,28},{1,5},{5,9},{9,... | collective-permute-start | bytes 786440 | tf_op jit(solution)/shard_map/while/body/eval_jaxpr/ppermute | solution.py:23
  145.3 12.3 %collective-permute-start.3 = (bf16[256,4,128]{2,0,1:T(8,128)(2,1)S(1)}, bf16[256,4,128]{2,0,1:T(8,128)(2,1)S(1)}, u32[]{:S(2)}, u32[]{:S(2)}) collective-permute-start(bf16[256,4,128]{2,0,1:T(8,128)(2,1)S(1)} %get-tuple-element.1077), channel_id=1, source_target_pairs={{0,4},{4,8},{8,12},{12,16},{16,20},{20,24},{24,28},{1,5},{5,9},{9,... | collective-permute-start | bytes 786440 | tf_op jit(solution)/shard_map/while/body/eval_jaxpr/ppermute | solution.py:23
  149.4 13.2 %collective-permute-start.4 = (bf16[256,4,128]{2,0,1:T(8,128)(2,1)}, bf16[256,4,128]{2,0,1:T(8,128)(2,1)S(1)}, u32[]{:S(2)}, u32[]{:S(2)}) collective-permute-start(bf16[256,4,128]{2,0,1:T(8,128)(2,1)} %get-tuple-element.1079), channel_id=1, source_target_pairs={{0,4},{4,8},{8,12},{12,16},{16,20},{20,24},{24,28},{28,0},{1,5},{5... | collective-permute-start | bytes 786440 | tf_op jit(solution)/shard_map/while/body/eval_jaxpr/ppermute | solution.py:28
  149.5 15.9 %collective-permute-start.5 = (bf16[256,4,128]{2,0,1:T(8,128)(2,1)}, bf16[256,4,128]{2,0,1:T(8,128)(2,1)S(1)}, u32[]{:S(2)}, u32[]{:S(2)}) collective-permute-start(bf16[256,4,128]{2,0,1:T(8,128)(2,1)} %get-tuple-element.1080), channel_id=1, source_target_pairs={{0,4},{4,8},{8,12},{12,16},{16,20},{20,24},{24,28},{28,0},{1,5},{5... | collective-permute-start | bytes 786440 | tf_op jit(solution)/shard_map/while/body/eval_jaxpr/ppermute | solution.py:28
  166.4 11.0 %collective-permute-start.2 = (bf16[256,4,128]{2,0,1:T(8,128)(2,1)S(1)}, bf16[256,4,128]{2,0,1:T(8,128)(2,1)S(1)}, u32[]{:S(2)}, u32[]{:S(2)}) collective-permute-start(bf16[256,4,128]{2,0,1:T(8,128)(2,1)S(1)} %get-tuple-element.1076), channel_id=1, source_target_pairs={{0,4},{4,8},{8,12},{12,16},{16,20},{20,24},{24,28},{1,5},{5,9},{9,... | collective-permute-start | bytes 786440 | tf_op jit(solution)/shard_map/while/body/eval_jaxpr/ppermute | solution.py:23
  170.7 12.3 %collective-permute-start.3 = (bf16[256,4,128]{2,0,1:T(8,128)(2,1)S(1)}, bf16[256,4,128]{2,0,1:T(8,128)(2,1)S(1)}, u32[]{:S(2)}, u32[]{:S(2)}) collective-permute-start(bf16[256,4,128]{2,0,1:T(8,128)(2,1)S(1)} %get-tuple-element.1077), channel_id=1, source_target_pairs={{0,4},{4,8},{8,12},{12,16},{16,20},{20,24},{24,28},{1,5},{5,9},{9,... | collective-permute-start | bytes 786440 | tf_op jit(solution)/shard_map/while/body/eval_jaxpr/ppermute | solution.py:23
  173.9 13.1 %collective-permute-start.4 = (bf16[256,4,128]{2,0,1:T(8,128)(2,1)}, bf16[256,4,128]{2,0,1:T(8,128)(2,1)S(1)}, u32[]{:S(2)}, u32[]{:S(2)}) collective-permute-start(bf16[256,4,128]{2,0,1:T(8,128)(2,1)} %get-tuple-element.1079), channel_id=1, source_target_pairs={{0,4},{4,8},{8,12},{12,16},{16,20},{20,24},{24,28},{28,0},{1,5},{5... | collective-permute-start | bytes 786440 | tf_op jit(solution)/shard_map/while/body/eval_jaxpr/ppermute | solution.py:28
  174.0 15.8 %collective-permute-start.5 = (bf16[256,4,128]{2,0,1:T(8,128)(2,1)}, bf16[256,4,128]{2,0,1:T(8,128)(2,1)S(1)}, u32[]{:S(2)}, u32[]{:S(2)}) collective-permute-start(bf16[256,4,128]{2,0,1:T(8,128)(2,1)} %get-tuple-element.1080), channel_id=1, source_target_pairs={{0,4},{4,8},{8,12},{12,16},{16,20},{20,24},{24,28},{28,0},{1,5},{5... | collective-permute-start | bytes 786440 | tf_op jit(solution)/shard_map/while/body/eval_jaxpr/ppermute | solution.py:28
  190.9 11.0 %collective-permute-start.2 = (bf16[256,4,128]{2,0,1:T(8,128)(2,1)S(1)}, bf16[256,4,128]{2,0,1:T(8,128)(2,1)S(1)}, u32[]{:S(2)}, u32[]{:S(2)}) collective-permute-start(bf16[256,4,128]{2,0,1:T(8,128)(2,1)S(1)} %get-tuple-element.1076), channel_id=1, source_target_pairs={{0,4},{4,8},{8,12},{12,16},{16,20},{20,24},{24,28},{1,5},{5,9},{9,... | collective-permute-start | bytes 786440 | tf_op jit(solution)/shard_map/while/body/eval_jaxpr/ppermute | solution.py:23
  195.2 12.3 %collective-permute-start.3 = (bf16[256,4,128]{2,0,1:T(8,128)(2,1)S(1)}, bf16[256,4,128]{2,0,1:T(8,128)(2,1)S(1)}, u32[]{:S(2)}, u32[]{:S(2)}) collective-permute-start(bf16[256,4,128]{2,0,1:T(8,128)(2,1)S(1)} %get-tuple-element.1077), channel_id=1, source_target_pairs={{0,4},{4,8},{8,12},{12,16},{16,20},{20,24},{24,28},{1,5},{5,9},{9,... | collective-permute-start | bytes 786440 | tf_op jit(solution)/shard_map/while/body/eval_jaxpr/ppermute | solution.py:23
  198.3 12.3 %collective-permute-start.4 = (bf16[256,4,128]{2,0,1:T(8,128)(2,1)}, bf16[256,4,128]{2,0,1:T(8,128)(2,1)S(1)}, u32[]{:S(2)}, u32[]{:S(2)}) collective-permute-start(bf16[256,4,128]{2,0,1:T(8,128)(2,1)} %get-tuple-element.1079), channel_id=1, source_target_pairs={{0,4},{4,8},{8,12},{12,16},{16,20},{20,24},{24,28},{28,0},{1,5},{5... | collective-permute-start | bytes 786440 | tf_op jit(solution)/shard_map/while/body/eval_jaxpr/ppermute | solution.py:28
  198.3 15.0 %collective-permute-start.5 = (bf16[256,4,128]{2,0,1:T(8,128)(2,1)}, bf16[256,4,128]{2,0,1:T(8,128)(2,1)S(1)}, u32[]{:S(2)}, u32[]{:S(2)}) collective-permute-start(bf16[256,4,128]{2,0,1:T(8,128)(2,1)} %get-tuple-element.1080), channel_id=1, source_target_pairs={{0,4},{4,8},{8,12},{12,16},{16,20},{20,24},{24,28},{28,0},{1,5},{5... | collective-permute-start | bytes 786440 | tf_op jit(solution)/shard_map/while/body/eval_jaxpr/ppermute | solution.py:28
  214.4 10.8 %collective-permute-start.7 = (bf16[256,4,128]{2,0,1:T(8,128)(2,1)}, bf16[256,4,128]{2,0,1:T(8,128)(2,1)S(1)}, u32[]{:S(2)}, u32[]{:S(2)}) collective-permute-start(bf16[256,4,128]{2,0,1:T(8,128)(2,1)} %get-tuple-element.607), channel_id=1, source_target_pairs={{0,20},{4,24},{8,28},{12,0},{16,4},{20,8},{24,12},{28,16},{1,21},{... | collective-permute-start | bytes 786440 | tf_op jit(solution)/shard_map/ppermute | solution.py:28
  215.3 0.9 copy-start.15
  216.2 77.2 %collective-permute-start.6 = (bf16[256,4,128]{2,0,1:T(8,128)(2,1)S(1)}, bf16[256,4,128]{2,0,1:T(8,128)(2,1)S(1)}, u32[]{:S(2)}, u32[]{:S(2)}) collective-permute-start(bf16[256,4,128]{2,0,1:T(8,128)(2,1)S(1)} %copy-done.15), channel_id=1, source_target_pairs={{0,20},{4,24},{8,28},{12,0},{16,4},{20,8},{24,12},{28,16},{1,21},{... | collective-permute-start | bytes 786440 | tf_op jit(solution)/shard_map/ppermute | solution.py:28
  293.5 0.9 copy-start.16
Sparse Core Ops, SparseCore 0:
  11.5 72.5 all-reduce.6
  215.4 75.8 all-reduce.4
where the time goes:
time: 303 us
  waiting for transfers between devices  182 us (60%)
  starting transfers between devices  59.1 us (20%)
  matrix products  21.1 us (7%)
  local copies, waits for them, and re-layouts  20.5 us (7%)
  between operations  14.4 us (5%)
  other arithmetic  5.12 us (2%)
    psum x1, waiting for transfers between devices, from_root(): return lax.psum(kept, axis)  69 us
    psum x1, waiting for transfers between devices, on_device(): prompt_dk, prompt_dv = lax.psum((prompt_dk, prompt_dv), 'ctx')  66.1 us
    ppermute x12, starting transfers between devices, passed_along(): return lax.ppermute(block, axis, route)  47.4 us
    ppermute x12, waiting for transfers between devices, passed_along(): return lax.ppermute(block, axis, route)  31.5 us
    ppermute x8, waiting for transfers between devices, shifted(): lax.ppermute(value, axis, [(i, (i + by) % length) for i in range(length)])  15.2 us
    unnamed x51, local copies, waits for them, and re-layouts  14.1 us
    ppermute x8, starting transfers between devices, shifted(): lax.ppermute(value, axis, [(i, (i + by) % length) for i in range(length)])  11.7 us
  transfers between devices with their start and end apart: 22, of which 20 were waited for; matrix products, arithmetic and copies ran while one was open for 7% of the time, Pallas kernels for 0%

commit v1 on v0

v1 whole, which is shorter than its diff:
```python
import functools
import math

import jax
import jax.numpy as jnp
from jax import lax
from jax.experimental import pallas as pl
from jax.experimental.pallas import tpu as pltpu
from jax.sharding import PartitionSpec as P

HD = 128
PROMPT = 64
DOC_MOST = 768
REACH = 3
NEG_FILL = -1e30
SCALE = 1.0 / math.sqrt(HD)
SCALE2 = SCALE * math.log2(math.e)
MESH = pl.DeviceIdType.MESH


def remote(src, dst, send_sem, recv_sem, target):
    return pltpu.make_async_remote_copy(
        src_ref=src,
        dst_ref=dst,
        send_sem=send_sem,
        recv_sem=recv_sem,
        device_id={"ctx": target},
        device_id_type=MESH,
    )


def dot_nt(a, b):
    return lax.dot_general(a, b, (((1,), (1,)), ((), ())), preferred_element_type=jnp.float32)


def dot_nn(a, b):
    return jnp.dot(a, b, preferred_element_type=jnp.float32)


def kernel(
    n, first, len_ref, q_ref, k_ref, v_ref, g_ref,
    att_ref, dq_ref, dk_ref, dv_ref,
    kv_buf, qd_buf, pr_buf, pg_out, pg_buf, ld_own, ld_buf,
    s_buf, sp_buf, top_ref, tot_ref, lse_ref, del_ref,
    kv_ss, kv_rs, qd_ss, qd_rs, ld_ss, ld_rs, pr_ss, pr_rs, pg_ss, pg_rs,
):
    rows, width = q_ref.shape
    heads = width // HD
    docs = len_ref.shape[0]
    me = lax.axis_index("ctx")
    later = n - first

    def has_before(d):
        return (me >= d) & ((me < first) | (me >= first + d))

    def has_after(d):
        return (me + d < n) & ((me + d < first) | (me >= first))

    barrier = pltpu.get_barrier_semaphore()
    for s in range(1, n):
        pl.semaphore_signal(
            barrier, inc=1, device_id={"ctx": lax.rem(me + s, n)}, device_id_type=MESH
        )
    pl.semaphore_wait(barrier, n - 1)

    chunks = ((0, PROMPT), (PROMPT, rows - PROMPT))

    def kv_copy(d, w, c):
        part = pl.ds(*chunks[c])
        src = (k_ref, v_ref)[w]
        return remote(
            src.at[part], kv_buf.at[d - 1, w, part], kv_ss.at[d - 1, w, c], kv_rs.at[d - 1, w, c],
            lax.rem(me + d, n),
        )

    def qd_copy(d, w):
        src = (q_ref, g_ref)[w]
        return remote(
            src, qd_buf.at[d - 1, w], qd_ss.at[d - 1, w], qd_rs.at[d - 1, w],
            lax.rem(me + n - d, n),
        )

    def ld_copy(d):
        return remote(
            ld_own, ld_buf.at[d - 1], ld_ss.at[d - 1], ld_rs.at[d - 1], lax.rem(me + n - d, n)
        )

    def pr_copy(src, w):
        return remote(src, pr_buf.at[w], pr_ss.at[w], pr_rs.at[w], lax.rem(me + 2, n))

    def pg_copy():
        slot = lax.rem(me + n - first, n)
        return remote(pg_out, pg_buf.at[slot], pg_ss, pg_rs.at[slot], 0)

    distances = range(1, REACH + 1)
    for c in (0, 1):
        for d in distances:
            @pl.when(has_after(d))
            def _(d=d, c=c):
                for w in (0, 1):
                    kv_copy(d, w, c).start()
    for d in distances:
        @pl.when(has_before(d))
        def _(d=d):
            for w in (0, 1):
                qd_copy(d, w).start()

    def doc_start(pos):
        start = jnp.zeros_like(pos)
        end = jnp.int32(0)
        for i in range(docs):
            end = end + len_ref[i]
            start = jnp.where(pos >= end, end, start)
        return start

    col = lax.broadcasted_iota(jnp.int32, (rows, 1), 0)
    row = lax.broadcasted_iota(jnp.int32, (1, rows), 1)
    t_col = me * rows + col
    ds_col = doc_start(t_col)

    def hs(h):
        return pl.ds(pl.multiple_of(h * HD, HD), HD)

    def row_forward(h, keys, values, mask):
        s = dot_nt(q_ref[:, hs(h)], keys) * SCALE2
        if mask is not None:
            s = jnp.where(mask, s, NEG_FILL)
        top = top_ref[h]
        fresh = jnp.maximum(top, jnp.max(s, axis=1, keepdims=True))
        fade = jnp.exp2(top - fresh)
        p = jnp.exp2(s - fresh)
        top_ref[h] = fresh
        tot_ref[h] = tot_ref[h] * fade + jnp.sum(p, axis=1, keepdims=True)
        att_ref[:, hs(h)] = att_ref[:, hs(h)] * fade + dot_nn(p.astype(jnp.bfloat16), values)
        return s

    own_mask = (row <= col) & (me * rows + row >= ds_col)

    @pl.loop(0, heads)
    def _(h):
        s = dot_nt(q_ref[:, hs(h)], k_ref[:, hs(h)]) * SCALE2
        s = jnp.where(own_mask, s, NEG_FILL)
        top = jnp.max(s, axis=1, keepdims=True)
        p = jnp.exp2(s - top)
        s_buf[0, h] = s
        top_ref[h] = top
        tot_ref[h] = jnp.sum(p, axis=1, keepdims=True)
        att_ref[:, hs(h)] = dot_nn(p.astype(jnp.bfloat16), v_ref[:, hs(h)])

    for holder in (first - 2, first - 1):
        @pl.when(me == holder)
        def _(holder=holder):
            for w in (0, 1):
                kv_copy(holder, w, 0).wait_recv()
                pr_copy(kv_buf.at[holder - 1, w, pl.ds(0, PROMPT)], w).start()

    @pl.when(me >= first)
    def _():
        for w in (0, 1):
            pr_copy(pr_buf.at[w], w).wait_recv()

        @pl.when(me + 2 < n)
        def _():
            for w in (0, 1):
                pr_copy(pr_buf.at[w], w).start()

        @pl.loop(0, heads)
        def _(h):
            sp_buf[h] = row_forward(h, pr_buf[0, :, hs(h)], pr_buf[1, :, hs(h)], None)

    for d in distances:
        @pl.when(has_before(d))
        def _(d=d):
            for w in (0, 1):
                for c in (0, 1):
                    if c == 0 and d in (first - 2, first - 1):
                        @pl.when(me != d)
                        def _(w=w):
                            kv_copy(d, w, 0).wait_recv()
                    else:
                        kv_copy(d, w, c).wait_recv()
            mask = (me - d) * rows + row >= ds_col

            @pl.loop(0, heads)
            def _(h):
                s_buf[d, h] = row_forward(
                    h, kv_buf[d - 1, 0, :, hs(h)], kv_buf[d - 1, 1, :, hs(h)], mask
                )

    @pl.loop(0, heads)
    def _(h):
        total = tot_ref[h]
        att = att_ref[:, hs(h)] / total
        att_ref[:, hs(h)] = att
        lse_ref[h] = top_ref[h] + jnp.log2(total)
        del_ref[h] = jnp.sum(att * g_ref[:, hs(h)].astype(jnp.float32), axis=1, keepdims=True)

    lane = lax.broadcasted_iota(jnp.int32, (rows, HD), 1)
    packed = jnp.zeros((rows, HD), jnp.float32)
    for h in range(heads):
        packed = jnp.where(lane == h, lse_ref[h], packed)
        packed = jnp.where(lane == heads + h, del_ref[h], packed)
    ld_own[...] = jnp.transpose(packed)[: 2 * heads]

    for d in distances:
        @pl.when(has_before(d))
        def _(d=d):
            ld_copy(d).start()

    def column(h, q, g, lse, delta, keys, values, mask):
        s = dot_nt(keys, q) * SCALE2
        if mask is not None:
            s = jnp.where(mask, s, NEG_FILL)
        p = jnp.exp2(s - lse)
        dp = dot_nt(values, g)
        ds = (p * (dp - delta)).astype(jnp.bfloat16)
        return dot_nn(ds, q), dot_nn(p.astype(jnp.bfloat16), g)

    @pl.when(me >= first)
    def _():
        @pl.loop(0, heads)
        def _(h):
            dk, dv = column(
                h, q_ref[:, hs(h)], g_ref[:, hs(h)],
                ld_own[pl.ds(h, 1)], ld_own[pl.ds(heads + h, 1)],
                pr_buf[0, :, hs(h)], pr_buf[1, :, hs(h)], None,
            )
            pg_out[0, :, hs(h)] = dk.astype(jnp.bfloat16)
            pg_out[1, :, hs(h)] = dv.astype(jnp.bfloat16)

        pg_copy().start()

    def row_backward(h, s, keys, values):
        p = jnp.exp2(s - lse_ref[h])
        dp = dot_nt(g_ref[:, hs(h)], values)
        ds = (p * (dp - del_ref[h])).astype(jnp.bfloat16)
        return dot_nn(ds, keys) * SCALE

    own_cols = (col <= row) & (me * rows + col >= doc_start(me * rows + row))

    @pl.loop(0, heads)
    def _(h):
        dq_ref[:, hs(h)] = row_backward(h, s_buf[0, h], k_ref[:, hs(h)], v_ref[:, hs(h)])
        dk, dv = column(
            h, q_ref[:, hs(h)], g_ref[:, hs(h)],
            ld_own[pl.ds(h, 1)], ld_own[pl.ds(heads + h, 1)],
            k_ref[:, hs(h)], v_ref[:, hs(h)], own_cols,
        )
        dk_ref[:, hs(h)] = dk
        dv_ref[:, hs(h)] = dv

    @pl.when(me >= first)
    def _():
        @pl.loop(0, heads)
        def _(h):
            dq_ref[:, hs(h)] += row_backward(
                h, sp_buf[h], pr_buf[0, :, hs(h)], pr_buf[1, :, hs(h)]
            )

    for d in distances:
        @pl.when(has_before(d))
        def _(d=d):
            @pl.loop(0, heads)
            def _(h):
                dq_ref[:, hs(h)] += row_backward(
                    h, s_buf[d, h], kv_buf[d - 1, 0, :, hs(h)], kv_buf[d - 1, 1, :, hs(h)]
                )

    for d in distances:
        @pl.when(has_after(d))
        def _(d=d):
            for w in (0, 1):
                qd_copy(d, w).wait_recv()
            ld_copy(d).wait_recv()
            mask = me * rows + col >= doc_start((me + d) * rows + row)

            @pl.loop(0, heads)
            def _(h):
                dk, dv = column(
                    h, qd_buf[d - 1, 0, :, hs(h)], qd_buf[d - 1, 1, :, hs(h)],
                    ld_buf[d - 1, pl.ds(h, 1)], ld_buf[d - 1, pl.ds(heads + h, 1)],
                    k_ref[:, hs(h)], v_ref[:, hs(h)], mask,
                )
                dk_ref[:, hs(h)] += dk
                dv_ref[:, hs(h)] += dv

    @pl.when(me == 0)
    def _():
        @pl.loop(0, later)
        def _(i):
            remote(pg_out, pg_buf.at[i], pg_ss, pg_rs.at[i], 0).wait_recv()
            dk_ref[pl.ds(0, PROMPT)] += pg_buf[i, 0].astype(jnp.float32)
            dv_ref[pl.ds(0, PROMPT)] += pg_buf[i, 1].astype(jnp.float32)

    dk_ref[...] = dk_ref[...] * SCALE

    for d in distances:
        @pl.when(has_after(d))
        def _(d=d):
            for w in (0, 1):
                for c in (0, 1):
                    kv_copy(d, w, c).wait_send()

        @pl.when(has_before(d))
        def _(d=d):
            for w in (0, 1):
                qd_copy(d, w).wait_send()
            ld_copy(d).wait_send()

    @pl.when((me >= first - 2) & (me + 2 < n))
    def _():
        for w in (0, 1):
            pr_copy(pr_buf.at[w], w).wait_send()

    @pl.when(me >= first)
    def _():
        pg_copy().wait_send()


def on_device(queries, keys, values, out_grad, doc_lengths):
    rows, width = queries.shape
    heads = width // HD
    n = lax.axis_size("ctx")
    first = DOC_MOST // rows
    later = n - first
    bf, f32 = jnp.bfloat16, jnp.float32
    vmem = pl.BlockSpec(memory_space=pltpu.VMEM)
    dma = pltpu.SemaphoreType.DMA
    tile = rows * rows * heads
    out = jax.ShapeDtypeStruct((rows, width), f32)
    return pl.pallas_call(
        functools.partial(kernel, n, first),
        out_shape=[out] * 4,
        in_specs=[pl.BlockSpec(memory_space=pltpu.SMEM)] + [vmem] * 4,
        out_specs=[vmem] * 4,
        scratch_shapes=[
            pltpu.VMEM((REACH, 2, rows, width), bf),
            pltpu.VMEM((REACH, 2, rows, width), bf),
            pltpu.VMEM((2, PROMPT, width), bf),
            pltpu.VMEM((2, PROMPT, width), bf),
            pltpu.VMEM((later, 2, PROMPT, width), bf),
            pltpu.VMEM((2 * heads, rows), f32),
            pltpu.VMEM((REACH, 2 * heads, rows), f32),
            pltpu.VMEM((REACH + 1, heads, rows, rows), f32),
            pltpu.VMEM((heads, rows, PROMPT), f32),
            pltpu.VMEM((heads, rows, 1), f32),
            pltpu.VMEM((heads, rows, 1), f32),
            pltpu.VMEM((heads, rows, 1), f32),
            pltpu.VMEM((heads, rows, 1), f32),
            dma((REACH, 2, 2)), dma((REACH, 2, 2)),
            dma((REACH, 2)), dma((REACH, 2)),
            dma((REACH,)), dma((REACH,)),
            dma((2,)), dma((2,)),
            dma(()), dma((later,)),
        ],
        compiler_params=pltpu.CompilerParams(
            collective_id=0, has_side_effects=True, vmem_limit_bytes=48 * 2**20
        ),
        cost_estimate=pl.CostEstimate(
            flops=2 * 8 * 4 * tile * HD, bytes_accessed=12 * rows * width, transcendentals=8 * tile
        ),
    )(doc_lengths, queries, keys, values, out_grad)


def solution(mesh):
    block = P("ctx", "head")
    return jax.shard_map(
        on_device, mesh=mesh, in_specs=(block,) * 4 + (P(),), out_specs=(block,) * 4, check_vma=False
    )
```

time: 303 us -> 77.6 us (0.26)
  waiting for transfers between devices: 182 us -> 0 us
  Pallas kernels: 0 us -> 69.1 us
  starting transfers between devices: 59.1 us -> 0 us
  matrix products: 21.1 us -> 0 us
  between operations: 14.4 us -> 0.65 us
  local copies, waits for them, and re-layouts: 20.5 us -> 7.62 us
  other arithmetic: 5.12 us -> 0 us
    psum x2 -> x0, waiting for transfers between devices: 135 us -> none  [the longest x1 69 us: from_root(): return lax.psum(kept, axis)]
    pallas_call x0 -> x1, Pallas kernels: none -> 69.1 us  [on_device(): pl.pallas_call(functools.partial(kernel, n, first), out_shape=[out] * 4,...]
    ppermute x20 -> x0, starting transfers between devices: 59 us -> none  [the longest x12 47.4 us: passed_along(): return lax.ppermute(block, axis, route)]
    ppermute x20 -> x0, waiting for transfers between devices: 46.7 us -> none  [the longest x12 31.5 us: passed_along(): return lax.ppermute(block, axis, route)]
    dot_general x33 -> x0, matrix products: 21.1 us -> none  [the longest x5 5.03 us: grad_scored(): jnp.einsum('htu,thd->uhd', rounded, dout_rows, preferred_element_type=jnp...]
    unnamed x51 -> x14, local copies, waits for them, and re-layouts: 14.1 us -> 7.62 us
    while x16 -> x0, local copies, waits for them, and re-layouts: 4.54 us -> none
  transfers between devices with their start and end apart: 22 -> 0, of which waited for: 20 -> 0; matrix products, arithmetic and copies ran while one was open for 7% -> 0% of each run, Pallas kernels for 0% -> 0%
where the time goes in v1:
time: 77.6 us; the launch traced here: 77.4 us
  Pallas kernels  69.1 us (89%)
  local copies, waits for them, and re-layouts  7.62 us (10%)
    pallas_call x1, Pallas kernels, on_device(): pl.pallas_call(functools.partial(kernel, n, first), out_shape=[out] * 4,...  69.1 us
    unnamed x14, local copies, waits for them, and re-layouts  7.62 us

profile of v1, /device:TPU:0, one launch (start us, length us, event | category | flops | bytes accessed | tf_op | source)
XLA Modules:
  0.0 77.4 jit_solution(16145446816024417938)
XLA Ops:
  0.6 0.0 copy-start
  0.6 0.9 %copy-done = bf16[256,512]{1,0:T(8,128)(2,1)S(1)} copy-done((bf16[256,512]{1,0:T(8,128)(2,1)S(1)}, bf16[256,512]{1,0:T(8,128)(2,1)}, u32[]{:S(2)}) %copy-start) | copy-done | bytes 262168
  1.6 0.0 copy-start.1
  1.6 0.9 %copy-done.1 = bf16[256,512]{1,0:T(8,128)(2,1)S(1)} copy-done((bf16[256,512]{1,0:T(8,128)(2,1)S(1)}, bf16[256,512]{1,0:T(8,128)(2,1)}, u32[]{:S(2)}) %copy-start.1) | copy-done | bytes 262168
  2.5 0.0 copy-start.2
  2.5 0.9 %copy-done.2 = bf16[256,512]{1,0:T(8,128)(2,1)S(1)} copy-done((bf16[256,512]{1,0:T(8,128)(2,1)S(1)}, bf16[256,512]{1,0:T(8,128)(2,1)}, u32[]{:S(2)}) %copy-start.2) | copy-done | bytes 262168
  3.5 0.0 copy-start.3
  3.5 0.9 %copy-done.3 = bf16[256,512]{1,0:T(8,128)(2,1)S(1)} copy-done((bf16[256,512]{1,0:T(8,128)(2,1)S(1)}, bf16[256,512]{1,0:T(8,128)(2,1)}, u32[]{:S(2)}) %copy-start.3) | copy-done | bytes 262168
  4.4 0.0 copy-start.4
  4.4 0.7 copy-done.4
  5.1 69.1 %shard_map.84 = (f32[256,512]{1,0:T(8,128)S(1)}, f32[256,512]{1,0:T(8,128)S(1)}, f32[256,512]{1,0:T(8,128)S(1)}, f32[256,512]{1,0:T(8,128)S(1)}) custom-call(s32[8]{0:T(128)S(1)} %copy-done.4, bf16[256,512]{1,0:T(8,128)(2,1)S(1)} %copy-done, bf16[256,512]{1,0:T(8,128)(2,1)S(1)} %copy-done.1, bf16[256,512]{1,0:T(8,128)(2,1)S(1)} %copy-done.2, ...), custom_call_target="tpu_custom_call" | custom-call | flops 2147483648 | bytes 1572864 | tf_op jit(solution)/shard_map/pallas_call | solution.py:331
  74.2 0.8 %copy.13 = f32[256,512]{1,0:T(8,128)} copy(f32[256,512]{1,0:T(8,128)S(1)} %get-tuple-element.8) | data formatting | bytes 1048576
  75.0 0.8 %copy.14 = f32[256,512]{1,0:T(8,128)} copy(f32[256,512]{1,0:T(8,128)S(1)} %get-tuple-element.9) | data formatting | bytes 1048576
  75.8 0.8 %copy.15 = f32[256,512]{1,0:T(8,128)} copy(f32[256,512]{1,0:T(8,128)S(1)} %get-tuple-element.10) | data formatting | bytes 1048576
  76.6 0.8 %copy.16 = f32[256,512]{1,0:T(8,128)} copy(f32[256,512]{1,0:T(8,128)S(1)} %get-tuple-element.11) | data formatting | bytes 1048576
Async XLA Ops:
  0.6 1.0 %copy-start = (bf16[256,512]{1,0:T(8,128)(2,1)S(1)}, bf16[256,512]{1,0:T(8,128)(2,1)}, u32[]{:S(2)}) copy-start(bf16[256,512]{1,0:T(8,128)(2,1)} %q_ref.1) | copy-start | bytes 786436
  1.6 0.9 %copy-start.1 = (bf16[256,512]{1,0:T(8,128)(2,1)S(1)}, bf16[256,512]{1,0:T(8,128)(2,1)}, u32[]{:S(2)}) copy-start(bf16[256,512]{1,0:T(8,128)(2,1)} %k_ref.1) | copy-start | bytes 786436
  2.5 0.9 %copy-start.2 = (bf16[256,512]{1,0:T(8,128)(2,1)S(1)}, bf16[256,512]{1,0:T(8,128)(2,1)}, u32[]{:S(2)}) copy-start(bf16[256,512]{1,0:T(8,128)(2,1)} %v_ref.1) | copy-start | bytes 786436
  3.5 0.9 %copy-start.3 = (bf16[256,512]{1,0:T(8,128)(2,1)S(1)}, bf16[256,512]{1,0:T(8,128)(2,1)}, u32[]{:S(2)}) copy-start(bf16[256,512]{1,0:T(8,128)(2,1)} %g_ref.1) | copy-start | bytes 786436
  4.4 0.7 copy-start.4
